TPU v7x, 512 devices: a whole 4x4x16 slice. The times are simulated.
512 devices in a mesh: phys: 2 (over x_hi), gx: 16 (over z), gy: 16 (over x_lo, y, core).
Axes of the slice: x: 4 (x_hi: 2, x_lo: 2; x = x_hi * 2 + x_lo), y: 4, z: 16, core: 2. Of those that a mesh axis runs over, the one named last changes fastest.
Arguments:
- models: float32 [2, 4, 1024, 2048], P('phys', None, 'gx', 'gy'), may hold values from -6 to 6
- channel_weight: float32 [2, 6], replicated, may hold values from 50 to 500
Outputs:
- gradient: float32 [2, 4, 1024, 2048], P('phys', None, 'gx', 'gy')
All inputs are finite; a program needn't handle non-finite values.
Results may differ from a plain program's by a relative error of at most 0.0001.
Values sent between devices are 32-bit elements; how exact they have to be, the bound alone decides.
No kernel may reach another device: no remote copies, remote signals or barrier semaphores. Data moves between devices by JAX's collectives and lax.ppermute only.
A program may use at most 64 MiB of HBM per device.

v0:
```python
import math
import jax
import jax.numpy as jnp
from jax import lax
from jax.sharding import PartitionSpec as P

gauss_total = sum((math.exp(-j * j / 50.0) for j in range(-15, 16)))


def extended(array, sides, width):
    for axis, dim in sides:
        peers, length = (lax.axis_size(axis), array.shape[dim])
        up = [(i, (i + 1) % peers) for i in range(peers - 1)]
        down = [(j, i) for i, j in up]
        last = lax.slice_in_dim(array, length - width, length, axis=dim)
        initial = lax.slice_in_dim(array, 0, width, axis=dim)
        before = lax.ppermute(last, axis, up)
        after = lax.ppermute(initial, axis, down)
        array = jnp.concatenate([before, array, after], axis=dim)
    return array


def from_partner(block, axis, stride):
    count = lax.axis_size(axis)
    route = []
    for low in range(count):
        high = low | 1 << stride
        if high != low and high < count:
            route += [(low, high), (high, low)]
    return lax.ppermute(block, axis, route)


def kernel_matrix(rows_n, cols_n, offset, dilation):
    row_index = lax.broadcasted_iota(jnp.int32, (rows_n, cols_n), 0)
    col_index = lax.broadcasted_iota(jnp.int32, (rows_n, cols_n), 1)
    distance = row_index - col_index + offset
    tap_index = distance // dilation
    on_tap = (distance == tap_index * dilation) & (jnp.abs(tap_index) <= 15)
    tap_float = tap_index.astype(jnp.float32)
    weights = jnp.exp(-tap_float * tap_float / 50.0) / gauss_total
    return jnp.where(on_tap, weights, 0.0)


def smooth_middle(values, dilation):
    lead, length, trail = values.shape
    highest = lax.Precision.HIGHEST
    if length <= 256:
        return jnp.einsum(
            "ij,ajb->aib", kernel_matrix(length, length, 0, dilation), values, precision=highest
        )
    block_count = length // 128
    blocks = values.reshape(lead, block_count, 128, trail)
    zero_block = jnp.zeros((lead, 1, 128, trail), values.dtype)
    after_blocks = jnp.concatenate([blocks[:, 1:], zero_block], 1)
    before_blocks = jnp.concatenate([zero_block, blocks[:, :-1]], 1)
    result = jnp.einsum(
        "ij,anjb->anib", kernel_matrix(128, 128, 0, dilation), blocks, precision=highest
    )
    result = result + jnp.einsum(
        "ij,anjb->anib", kernel_matrix(128, 128, -128, dilation), after_blocks, precision=highest
    )
    result = result + jnp.einsum(
        "ij,anjb->anib", kernel_matrix(128, 128, 128, dilation), before_blocks, precision=highest
    )
    return result.reshape(lead, length, trail)


def smooth_last(values, dilation):
    lead, trail, length = values.shape
    highest = lax.Precision.HIGHEST
    block_count = length // 128
    blocks = values.reshape(lead, trail, block_count, 128)
    zero_block = jnp.zeros((lead, trail, 1, 128), values.dtype)
    after_blocks = jnp.concatenate([blocks[:, :, 1:], zero_block], 2)
    before_blocks = jnp.concatenate([zero_block, blocks[:, :, :-1]], 2)
    result = jnp.einsum(
        "ajnk,ik->ajni", blocks, kernel_matrix(128, 128, 0, dilation), precision=highest
    )
    result = result + jnp.einsum(
        "ajnk,ik->ajni", after_blocks, kernel_matrix(128, 128, -128, dilation), precision=highest
    )
    result = result + jnp.einsum(
        "ajnk,ik->ajni", before_blocks, kernel_matrix(128, 128, 128, dilation), precision=highest
    )
    return result.reshape(lead, trail, length)


def smooth_rows(row_stack):
    row_count, x_cells, y_cells = row_stack.shape
    half_rows = row_count // 2
    depth_cells = row_count // 12
    z_rows = row_stack.reshape(12, depth_cells, x_cells * y_cells)
    z_done = jnp.concatenate([smooth_middle(z_rows[:6], 1), smooth_middle(z_rows[6:], 4)], 0)
    z_done = z_done.reshape(row_count, x_cells, y_cells)
    per_device = row_count // lax.axis_size("gx")
    dilation = jnp.where(lax.axis_index("gx") * per_device >= half_rows, 4, 1)
    x_done = lax.all_to_all(
        smooth_middle(
            lax.all_to_all(z_done, "gx", split_axis=0, concat_axis=1, tiled=True), dilation
        ),
        "gx",
        split_axis=1,
        concat_axis=0,
        tiled=True,
    )
    per_column = row_count // lax.axis_size("gy")
    dilation = jnp.where(lax.axis_index("gy") * per_column >= half_rows, 4, 1)
    return lax.all_to_all(
        smooth_last(
            lax.all_to_all(x_done, "gy", split_axis=0, concat_axis=2, tiled=True), dilation
        ),
        "gy",
        split_axis=2,
        concat_axis=0,
        tiled=True,
    )


def shards(models, channel_weight):
    model_field = models[0]
    depth_cells, x_cells, y_cells = model_field.shape
    padded = extended(model_field, (("gx", 1), ("gy", 2)), 1)
    z_padded = jnp.pad(model_field, ((1, 1), (0, 0), (0, 0)))
    slope_x = 0.5 * (padded[:, 2:, 1:-1] - padded[:, :-2, 1:-1])
    slope_y = 0.5 * (padded[:, 1:-1, 2:] - padded[:, 1:-1, :-2])
    slope_z = 0.5 * (z_padded[2:] - z_padded[:-2])
    tensor = jnp.stack(
        [
            slope_x * slope_x,
            slope_y * slope_y,
            slope_z * slope_z,
            slope_x * slope_y,
            slope_x * slope_z,
            slope_y * slope_z,
        ],
        0,
    )
    row_stack = jnp.concatenate([tensor, tensor], 0).reshape(12 * depth_cells, x_cells, y_cells)
    smoothed = smooth_rows(row_stack)
    partner_part = from_partner(smoothed, "phys", 0)
    weights = jnp.repeat(channel_weight.reshape(12), depth_cells)[:, None, None]
    adjoint = smooth_rows((smoothed - partner_part) * weights)
    half_rows = 6 * depth_cells
    combined = (adjoint[:half_rows] + adjoint[half_rows:]).reshape(6, depth_cells, x_cells, y_cells)
    q_x = 2.0 * combined[0] * slope_x + combined[3] * slope_y + combined[4] * slope_z
    q_y = 2.0 * combined[1] * slope_y + combined[3] * slope_x + combined[5] * slope_z
    q_z = 2.0 * combined[2] * slope_z + combined[4] * slope_x + combined[5] * slope_y
    lateral = extended(jnp.stack([q_x, q_y], 0), (("gx", 2), ("gy", 3)), 1)
    pad_z = jnp.pad(q_z, ((1, 1), (0, 0), (0, 0)))
    result = 0.5 * (lateral[0, :, :-2, 1:-1] - lateral[0, :, 2:, 1:-1])
    result = result + 0.5 * (lateral[1, :, 1:-1, :-2] - lateral[1, :, 1:-1, 2:])
    result = result + 0.5 * (pad_z[:-2] - pad_z[2:])
    return result[None]


def solution(mesh):
    in_specs = (P("phys", None, "gx", "gy"), P())
    out_specs = P("phys", None, "gx", "gy")
    return jax.shard_map(shards, mesh=mesh, in_specs=in_specs, out_specs=out_specs, check_vma=False)
```

profile of v0, /device:TPU:25, one launch (start us, length us, event | category | flops | bytes accessed | tf_op | source)
XLA Modules:
  0.0 646.8 jit_solution(4827848419836089784)
XLA Ops:
  2.1 4.2 collective-permute-start.1
  8.0 3.5 collective-permute-start.2
  11.6 4.1 collective-permute-start.3
  19.7 1.5 convolution_bitcast_fusion.2
  21.2 1.5 convolution_bitcast_fusion.3
  23.0 2.3 reshape.70
  25.3 16.5 %all-to-all-start = ((f32[48,64,128]{2,1,0:T(8,128)}), f32[48,64,128]{2,1,0:T(8,128)S(1)}, u32[]{:S(2)}, u32[]{:S(2)}) async-start(f32[48,64,128]{2,1,0:T(8,128)} %reshape.70), calls=%async_computation | async-start | bytes 3145728 | tf_op jit(solution)/shard_map/all_to_all | solution.py:99
  41.8 68.9 %all-to-all-done = f32[48,64,128]{2,1,0:T(8,128)S(1)} async-done(((f32[48,64,128]{2,1,0:T(8,128)}), f32[48,64,128]{2,1,0:T(8,128)S(1)}, u32[]{:S(2)}, u32[]{:S(2)}) %all-to-all-start) | async-done | bytes 1572896 | tf_op jit(solution)/shard_map/all_to_all | solution.py:99
  110.8 2.0 fusion.16
  112.8 2.2 fusion.102
  115.0 2.3 add_add_fusion.3
  118.4 101.6 %all_to_all.129 = f32[3,1024,128]{2,0,1:T(4,128)S(1)} all-to-all(f32[3,1024,128]{2,0,1:T(4,128)S(1)} %copy.22), channel_id=1, replica_groups=mesh['phys'=2,'gx'=16,'gy'=16] {'gx'}, dimensions={1} | all-to-all | bytes 3145728 | tf_op jit(solution)/shard_map/all_to_all | solution.py:97
  221.5 12.1 %all-to-all-start.2 = ((f32[48,64,128]{2,1,0:T(8,128)}), f32[48,64,128]{2,1,0:T(8,128)S(1)}, u32[]{:S(2)}, u32[]{:S(2)}) async-start(f32[48,64,128]{2,1,0:T(8,128)} %bitcast.19), calls=%async_computation.2 | async-start | bytes 3145728 | tf_op jit(solution)/shard_map/all_to_all | solution.py:110
  233.6 22.0 %all-to-all-done.2 = f32[48,64,128]{2,1,0:T(8,128)S(1)} async-done(((f32[48,64,128]{2,1,0:T(8,128)}), f32[48,64,128]{2,1,0:T(8,128)S(1)}, u32[]{:S(2)}, u32[]{:S(2)}) %all-to-all-start.2) | async-done | bytes 1572896 | tf_op jit(solution)/shard_map/all_to_all | solution.py:110
  256.8 2.9 fusion.98
  259.7 2.1 fusion.4
  261.9 2.1 add_add_fusion.2
  264.0 2.7 copy.41
  266.7 5.4 reshape.87
  272.1 24.6 %all_to_all.130 = f32[16,1,24576]{2,1,0:T(1,128)S(1)} all-to-all(f32[16,1,24576]{2,1,0:T(1,128)S(1)} %reshape.87), channel_id=1, replica_groups=mesh['phys'=2,'gx'=16,'gy'=16] {'gy'}, dimensions={0} | all-to-all | bytes 3145728 | tf_op jit(solution)/shard_map/all_to_all | solution.py:108
  297.2 4.4 reduce
  301.7 3.7 reshape.88
  305.4 3.3 copy.27
  308.7 4.6 collective-permute-start.4
  315.4 32.5 %collective-permute-done.4 = f32[48,64,128]{2,1,0:T(8,128)S(1)} collective-permute-done((f32[48,64,128]{2,1,0:T(8,128)S(1)}, f32[48,64,128]{2,1,0:T(8,128)S(1)}, u32[]{:S(2)}, u32[]{:S(2)}) %collective-permute-start.4) | collective-permute-done | bytes 1572896 | tf_op jit(solution)/shard_map/ppermute | solution.py:30
  349.2 1.5 convolution_bitcast_fusion
  351.0 1.5 convolution_bitcast_fusion.1
  354.0 73.7 %all_to_all.131 = f32[48,64,128]{2,1,0:T(8,128)S(1)} all-to-all(f32[48,64,128]{2,1,0:T(8,128)S(1)} %reshape.75), channel_id=1, replica_groups=mesh['phys'=2,'gx'=16,'gy'=16] {'gx'}, dimensions={0} | all-to-all | bytes 3145728 | tf_op jit(solution)/shard_map/all_to_all | solution.py:99
  427.8 2.0 fusion.13
  429.8 2.2 fusion.100
  432.0 2.3 add_add_fusion.1
  435.5 102.2 %all_to_all.132 = f32[3,1024,128]{2,0,1:T(4,128)S(1)} all-to-all(f32[3,1024,128]{2,0,1:T(4,128)S(1)} %copy.29), channel_id=1, replica_groups=mesh['phys'=2,'gx'=16,'gy'=16] {'gx'}, dimensions={1} | all-to-all | bytes 3145728 | tf_op jit(solution)/shard_map/all_to_all | solution.py:97
  537.9 31.8 %all_to_all.133 = f32[48,64,128]{2,1,0:T(8,128)S(1)} all-to-all(f32[48,64,128]{2,1,0:T(8,128)S(1)} %bitcast.139), channel_id=1, replica_groups=mesh['phys'=2,'gx'=16,'gy'=16] {'gy'}, dimensions={0} | all-to-all | bytes 3145728 | tf_op jit(solution)/shard_map/all_to_all | solution.py:110
  570.6 2.9 fusion.96
  573.8 2.1 fusion
  575.9 2.2 add_add_fusion
  578.2 2.7 copy.42
  580.9 5.4 reshape.89
  586.3 24.9 %all_to_all.134 = f32[16,1,24576]{2,1,0:T(1,128)S(1)} all-to-all(f32[16,1,24576]{2,1,0:T(1,128)S(1)} %reshape.89), channel_id=1, replica_groups=mesh['phys'=2,'gx'=16,'gy'=16] {'gy'}, dimensions={0} | all-to-all | bytes 3145728 | tf_op jit(solution)/shard_map/all_to_all | solution.py:108
  611.2 4.4 reduce.1
  615.6 3.7 reshape.90
  619.3 2.8 slice_add_fusion
  622.9 2.7 collective-permute-start.5
  627.0 3.0 collective-permute-done.6
  630.2 5.4 collective-permute-start.7
  635.6 1.9 collective-permute-start.8
  637.5 1.7 collective-permute-done.7
  639.2 6.5 %collective-permute-done.8 = f32[2,4,66,1]{3,2,1,0:T(8,128)S(1)} collective-permute-done((f32[2,4,66,1]{3,2,1,0:T(8,128)S(1)}, f32[2,4,66,1]{3,2,1,0:T(8,128)S(1)}, u32[]{:S(2)}, u32[]{:S(2)}) %collective-permute-start.8) | collective-permute-done | bytes 2144 | tf_op jit(solution)/shard_map/ppermute | solution.py:18
  (58 shorter events, 23.3 us)
Async XLA Ops:
  0.0 19.1 %copy-start = (f32[1,4,64,128]{3,2,1,0:T(8,128)S(1)}, f32[1,4,64,128]{3,2,1,0:T(8,128)}, u32[]{:S(2)}) copy-start(f32[1,4,64,128]{3,2,1,0:T(8,128)} %param.2) | copy-start | bytes 393220
  0.8 5.5 collective-permute-start
  2.1 4.9 collective-permute-start.1
  8.0 8.6 %collective-permute-start.2 = (f32[4,66,1]{2,1,0:T(8,128)S(1)}, f32[4,66,1]{2,1,0:T(8,128)S(1)}, u32[]{:S(2)}, u32[]{:S(2)}) collective-permute-start(f32[4,66,1]{2,1,0:T(8,128)S(1)} %get-tuple-element.24), channel_id=1, source_target_pairs={{1,0},{2,1},{3,2},{4,3},{5,4},{6,5},{7,6},{8,7},{9,8},{10,9},{11,1... | collective-permute-start | bytes 3176 | tf_op jit(solution)/shard_map/ppermute | solution.py:18
  11.6 6.2 collective-permute-start.3
  25.3 85.4 %all-to-all-start = ((f32[48,64,128]{2,1,0:T(8,128)}), f32[48,64,128]{2,1,0:T(8,128)S(1)}, u32[]{:S(2)}, u32[]{:S(2)}) async-start(f32[48,64,128]{2,1,0:T(8,128)} %reshape.70), calls=%async_computation | async-start | bytes 3145728 | tf_op jit(solution)/shard_map/all_to_all | solution.py:99
  221.5 34.1 %all-to-all-start.2 = ((f32[48,64,128]{2,1,0:T(8,128)}), f32[48,64,128]{2,1,0:T(8,128)S(1)}, u32[]{:S(2)}, u32[]{:S(2)}) async-start(f32[48,64,128]{2,1,0:T(8,128)} %bitcast.19), calls=%async_computation.2 | async-start | bytes 3145728 | tf_op jit(solution)/shard_map/all_to_all | solution.py:110
  305.3 7.9 %copy-start.1 = (f32[2,6]{1,0:T(2,128)S(1)}, f32[2,6]{1,0:T(2,128)}, u32[]{:S(2)}) copy-start(f32[2,6]{1,0:T(2,128)} %param.3) | copy-start | bytes 148
  308.7 39.2 %collective-permute-start.4 = (f32[48,64,128]{2,1,0:T(8,128)S(1)}, f32[48,64,128]{2,1,0:T(8,128)S(1)}, u32[]{:S(2)}, u32[]{:S(2)}) collective-permute-start(f32[48,64,128]{2,1,0:T(8,128)S(1)} %bitcast.133), channel_id=1, source_target_pairs={{0,256},{256,0},{1,257},{257,1},{2,258},{258,2},{3,259},{259,3},{4... | collective-permute-start | bytes 4718600 | tf_op jit(solution)/shard_map/ppermute | solution.py:30
  622.9 4.0 collective-permute-start.5
  625.6 4.4 collective-permute-start.6
  630.2 9.1 %collective-permute-start.7 = (f32[2,4,66,1]{3,2,1,0:T(8,128)S(1)}, f32[2,4,66,1]{3,2,1,0:T(8,128)S(1)}, u32[]{:S(2)}, u32[]{:S(2)}) collective-permute-start(f32[2,4,66,1]{3,2,1,0:T(8,128)S(1)} %get-tuple-element.16), channel_id=1, source_target_pairs={{0,1},{1,2},{2,3},{3,4},{4,5},{5,6},{6,7},{7,8},{8,9},{9,10},{10,1... | collective-permute-start | bytes 6344 | tf_op jit(solution)/shard_map/ppermute | solution.py:17
  635.6 10.2 %collective-permute-start.8 = (f32[2,4,66,1]{3,2,1,0:T(8,128)S(1)}, f32[2,4,66,1]{3,2,1,0:T(8,128)S(1)}, u32[]{:S(2)}, u32[]{:S(2)}) collective-permute-start(f32[2,4,66,1]{3,2,1,0:T(8,128)S(1)} %get-tuple-element.17), channel_id=1, source_target_pairs={{1,0},{2,1},{3,2},{4,3},{5,4},{6,5},{7,6},{8,7},{9,8},{10,9},{11,1... | collective-permute-start | bytes 6344 | tf_op jit(solution)/shard_map/ppermute | solution.py:18
where the time goes:
time: 652 us; the launch traced here: 647 us
  blocking collectives  359 us (55%)
  waiting for transfers between devices  137 us (21%)
  starting transfers between devices  57.6 us (9%)
  local copies, waits for them, and re-layouts  42.1 us (6%)
  matrix products  33.3 us (5%)
  other arithmetic  16.6 us (3%)
    all_to_all x2, blocking collectives, smooth_rows(): lax.all_to_all(smooth_middle(lax.all_to_all(z_done, 'gx', split_axis=0, c...  204 us
    all_to_all x1, blocking collectives, smooth_rows(): lax.all_to_all(z_done, 'gx', split_axis=0, concat_axis=1, tiled=True)  73.7 us
    all_to_all x1, waiting for transfers between devices, smooth_rows(): lax.all_to_all(z_done, 'gx', split_axis=0, concat_axis=1, tiled=True)  68.9 us
    all_to_all x2, blocking collectives, smooth_rows(): lax.all_to_all(smooth_last(lax.all_to_all(x_done, 'gy', split_axis=0, con...  49.4 us
    ppermute x1, waiting for transfers between devices, from_partner(): return lax.ppermute(block, axis, route)  32.5 us
    all_to_all x1, blocking collectives, smooth_rows(): lax.all_to_all(x_done, 'gy', split_axis=0, concat_axis=2, tiled=True)  31.8 us
    all_to_all x1, waiting for transfers between devices, smooth_rows(): lax.all_to_all(x_done, 'gy', split_axis=0, concat_axis=2, tiled=True)  22 us
    unnamed x13, local copies, waits for them, and re-layouts  18.4 us
  transfers between devices with their start and end apart: 11, of which 9 were waited for; matrix products, arithmetic and copies ran while one was open for 0% of the time, Pallas kernels for 0%

commit v1 on v0

--- a/solution.py
+++ b/solution.py
@@ -5,6 +5,28 @@
 from jax.sharding import PartitionSpec as P
 
 gauss_total = sum((math.exp(-j * j / 50.0) for j in range(-15, 16)))
+
+
+def cut_along(value, dim, size):
+    before, after = (value.shape[:dim], value.shape[dim + 1 :])
+    return jnp.moveaxis(value.reshape(*before, size, -1, *after), dim, 0)
+
+
+def in_order(tiles, dim):
+    tiles = jnp.moveaxis(tiles, 0, dim)
+    shape = tiles.shape
+    return tiles.reshape(*shape[:dim], shape[dim] * shape[dim + 1], *shape[dim + 2 :])
+
+
+def sent_to_each(x, axis, split_dim, concat_dim):
+    length, place = (lax.axis_size(axis), lax.axis_index(axis))
+    blocks = cut_along(x, split_dim, length)
+    gathered = [blocks[place]]
+    for step in range(1, length):
+        sent = blocks[(place + step) % length]
+        gathered.append(lax.ppermute(sent, axis, [(i, (i + step) % length) for i in range(length)]))
+    blocks = jnp.stack(gathered)[(place - jnp.arange(length)) % length]
+    return in_order(blocks, concat_dim)
 
 
 def extended(array, sides, width):
@@ -94,14 +116,13 @@
     z_done = z_done.reshape(row_count, x_cells, y_cells)
     per_device = row_count // lax.axis_size("gx")
     dilation = jnp.where(lax.axis_index("gx") * per_device >= half_rows, 4, 1)
-    x_done = lax.all_to_all(
+    x_done = sent_to_each(
         smooth_middle(
             lax.all_to_all(z_done, "gx", split_axis=0, concat_axis=1, tiled=True), dilation
         ),
         "gx",
-        split_axis=1,
-        concat_axis=0,
-        tiled=True,
+        1,
+        0,
     )
     per_column = row_count // lax.axis_size("gy")
     dilation = jnp.where(lax.axis_index("gy") * per_column >= half_rows, 4, 1)

time: 652 us -> 665 us (1.020)
  blocking collectives: 359 us -> 150 us
  starting transfers between devices: 57.6 us -> 209 us
  waiting for transfers between devices: 137 us -> 207 us
    all_to_all x2 -> x0, blocking collectives: 204 us -> none  [smooth_rows(): lax.all_to_all(smooth_middle(lax.all_to_all(z_done, 'gx', split_axis=0, c...]
    ppermute x0 -> x30, starting transfers between devices: none -> 158 us  [sent_to_each(): lax.ppermute(sent, axis, [(i, (i + step) % length) for i in range(length)])]
    ppermute x0 -> x30, waiting for transfers between devices: none -> 69.5 us  [sent_to_each(): lax.ppermute(sent, axis, [(i, (i + step) % length) for i in range(length)])]
    unnamed x13 -> x45, local copies, waits for them, and re-layouts: 18.4 us -> 18.7 us
  transfers between devices with their start and end apart: 11 -> 41, of which waited for: 9 -> 22; matrix products, arithmetic and copies ran while one was open for 0% -> 0% of each run, Pallas kernels for 0% -> 0%
where the time goes in v1:
time: 665 us; the launch traced here: 659 us
  starting transfers between devices  209 us (31%)
  waiting for transfers between devices  207 us (31%)
  blocking collectives  150 us (23%)
  local copies, waits for them, and re-layouts  41.5 us (6%)
  matrix products  33.2 us (5%)
  other arithmetic  16.4 us (2%)
    ppermute x30, starting transfers between devices, sent_to_each(): lax.ppermute(sent, axis, [(i, (i + step) % length) for i in range(length)])  158 us
    all_to_all x1, blocking collectives, smooth_rows(): lax.all_to_all(z_done, 'gx', split_axis=0, concat_axis=1, tiled=True)  74.2 us
    ppermute x30, waiting for transfers between devices, sent_to_each(): lax.ppermute(sent, axis, [(i, (i + step) % length) for i in range(length)])  69.5 us
    all_to_all x1, waiting for transfers between devices, smooth_rows(): lax.all_to_all(z_done, 'gx', split_axis=0, concat_axis=1, tiled=True)  68.7 us
    all_to_all x2, blocking collectives, smooth_rows(): lax.all_to_all(smooth_last(lax.all_to_all(x_done, 'gy', split_axis=0, con...  49.4 us
    ppermute x1, waiting for transfers between devices, from_partner(): return lax.ppermute(block, axis, route)  32.6 us
    all_to_all x1, blocking collectives, smooth_rows(): lax.all_to_all(x_done, 'gy', split_axis=0, concat_axis=2, tiled=True)  26.4 us
    all_to_all x1, waiting for transfers between devices, smooth_rows(): lax.all_to_all(x_done, 'gy', split_axis=0, concat_axis=2, tiled=True)  22 us
  transfers between devices with their start and end apart: 41, of which 22 were waited for; matrix products, arithmetic and copies ran while one was open for 0% of the time, Pallas kernels for 0%

profile of v1, /device:TPU:25, one launch (start us, length us, event | category | flops | bytes accessed | tf_op | source)
XLA Modules:
  0.0 658.8 jit_solution(1457150500149314450)
XLA Ops:
  2.1 4.2 collective-permute-start.1
  11.6 4.1 collective-permute-start.3
  25.3 16.5 %all-to-all-start = ((f32[48,64,128]{2,1,0:T(8,128)}), f32[48,64,128]{2,1,0:T(8,128)S(1)}, u32[]{:S(2)}, u32[]{:S(2)}) async-start(f32[48,64,128]{2,1,0:T(8,128)} %reshape.181), calls=%async_computation | async-start | bytes 3145728 | tf_op jit(solution)/shard_map/all_to_all | solution.py:121
  42.0 68.7 %all-to-all-done = f32[48,64,128]{2,1,0:T(8,128)S(1)} async-done(((f32[48,64,128]{2,1,0:T(8,128)}), f32[48,64,128]{2,1,0:T(8,128)S(1)}, u32[]{:S(2)}, u32[]{:S(2)}) %all-to-all-start) | async-done | bytes 1572896 | tf_op jit(solution)/shard_map/all_to_all | solution.py:121
  120.4 4.6 collective-permute-start.5
  125.1 6.0 collective-permute-start.6
  131.0 6.1 collective-permute-start.7
  139.1 8.5 %collective-permute-start.9 = (f32[3,64,128]{2,1,0:T(8,128)S(1)}, f32[3,64,128]{2,1,0:T(8,128)S(1)}, u32[]{:S(2)}, u32[]{:S(2)}) collective-permute-start(f32[3,64,128]{2,1,0:T(8,128)S(1)} %get-tuple-element.38), channel_id=1, source_target_pairs={{0,96},{16,112},{32,128},{48,144},{64,160},{80,176},{96,192},{112,... | collective-permute-start | bytes 294920 | tf_op jit(solution)/shard_map/ppermute | solution.py:27
  147.6 5.5 collective-permute-start.10
  153.1 6.4 collective-permute-start.11
  159.6 6.6 %collective-permute-start.12 = (f32[3,64,128]{2,1,0:T(8,128)S(1)}, f32[3,64,128]{2,1,0:T(8,128)S(1)}, u32[]{:S(2)}, u32[]{:S(2)}) collective-permute-start(f32[3,64,128]{2,1,0:T(8,128)S(1)} %get-tuple-element.35), channel_id=1, source_target_pairs={{0,144},{16,160},{32,176},{48,192},{64,208},{80,224},{96,240},{112... | collective-permute-start | bytes 294920 | tf_op jit(solution)/shard_map/ppermute | solution.py:27
  166.3 9.4 %collective-permute-start.13 = (f32[3,64,128]{2,1,0:T(8,128)S(1)}, f32[3,64,128]{2,1,0:T(8,128)S(1)}, u32[]{:S(2)}, u32[]{:S(2)}) collective-permute-start(f32[3,64,128]{2,1,0:T(8,128)S(1)} %get-tuple-element.34), channel_id=1, source_target_pairs={{0,160},{16,176},{32,192},{48,208},{64,224},{80,240},{96,0},{112,1... | collective-permute-start | bytes 294920 | tf_op jit(solution)/shard_map/ppermute | solution.py:27
  178.5 12.1 %collective-permute-start.15 = (f32[3,64,128]{2,1,0:T(8,128)S(1)}, f32[3,64,128]{2,1,0:T(8,128)S(1)}, u32[]{:S(2)}, u32[]{:S(2)}) collective-permute-start(f32[3,64,128]{2,1,0:T(8,128)S(1)} %get-tuple-element.32), channel_id=1, source_target_pairs={{0,192},{16,208},{32,224},{48,240},{64,0},{80,16},{96,32},{112,48}... | collective-permute-start | bytes 294920 | tf_op jit(solution)/shard_map/ppermute | solution.py:27
  190.7 5.2 collective-permute-start.16
  195.9 4.1 collective-permute-start.17
  200.1 6.9 %collective-permute-start.18 = (f32[3,64,128]{2,1,0:T(8,128)S(1)}, f32[3,64,128]{2,1,0:T(8,128)S(1)}, u32[]{:S(2)}, u32[]{:S(2)}) collective-permute-start(f32[3,64,128]{2,1,0:T(8,128)S(1)} %get-tuple-element.29), channel_id=1, source_target_pairs={{0,240},{16,0},{32,16},{48,32},{64,48},{80,64},{96,80},{112,96},{1... | collective-permute-start | bytes 294920 | tf_op jit(solution)/shard_map/ppermute | solution.py:27
  209.9 9.1 %collective-permute-done.15 = f32[3,64,128]{2,1,0:T(8,128)S(1)} collective-permute-done((f32[3,64,128]{2,1,0:T(8,128)S(1)}, f32[3,64,128]{2,1,0:T(8,128)S(1)}, u32[]{:S(2)}, u32[]{:S(2)}) %collective-permute-start.15) | collective-permute-done | bytes 98336 | tf_op jit(solution)/shard_map/ppermute | solution.py:27
  219.0 5.4 collective-permute-done.16
  224.4 4.2 collective-permute-done.17
  232.7 6.3 all-to-all-start.1
  239.0 22.0 %all-to-all-done.1 = f32[48,64,128]{2,1,0:T(8,128)S(1)} async-done(((f32[48,64,128]{2,1,0:T(8,128)}), f32[48,64,128]{2,1,0:T(8,128)S(1)}, u32[]{:S(2)}, u32[]{:S(2)}) %all-to-all-start.1) | async-done | bytes 1572896 | tf_op jit(solution)/shard_map/all_to_all | solution.py:131
  272.1 5.4 reshape.214
  277.5 24.6 %all_to_all.93 = f32[16,1,24576]{2,1,0:T(1,128)S(1)} all-to-all(f32[16,1,24576]{2,1,0:T(1,128)S(1)} %reshape.214), channel_id=1, replica_groups=mesh['phys'=2,'gx'=16,'gy'=16] {'gy'}, dimensions={0} | all-to-all | bytes 3145728 | tf_op jit(solution)/shard_map/all_to_all | solution.py:129
  302.6 4.3 reduce
  314.0 4.6 collective-permute-start.19
  320.6 32.6 %collective-permute-done.19 = f32[48,64,128]{2,1,0:T(8,128)S(1)} collective-permute-done((f32[48,64,128]{2,1,0:T(8,128)S(1)}, f32[48,64,128]{2,1,0:T(8,128)S(1)}, u32[]{:S(2)}, u32[]{:S(2)}) %collective-permute-start.19) | collective-permute-done | bytes 1572896 | tf_op jit(solution)/shard_map/ppermute | solution.py:52
  359.3 74.2 %all_to_all.94 = f32[48,64,128]{2,1,0:T(8,128)S(1)} all-to-all(f32[48,64,128]{2,1,0:T(8,128)S(1)} %reshape.186), channel_id=1, replica_groups=mesh['phys'=2,'gx'=16,'gy'=16] {'gx'}, dimensions={0} | all-to-all | bytes 3145728 | tf_op jit(solution)/shard_map/all_to_all | solution.py:121
  440.3 5.0 collective-permute-start.20
  445.3 4.9 collective-permute-start.21
  450.2 5.4 collective-permute-start.22
  455.5 4.4 collective-permute-start.23
  460.0 4.4 collective-permute-start.24
  464.4 7.7 %collective-permute-start.25 = (f32[3,64,128]{2,1,0:T(8,128)S(1)}, f32[3,64,128]{2,1,0:T(8,128)S(1)}, u32[]{:S(2)}, u32[]{:S(2)}) collective-permute-start(f32[3,64,128]{2,1,0:T(8,128)S(1)} %get-tuple-element.19), channel_id=1, source_target_pairs={{0,96},{16,112},{32,128},{48,144},{64,160},{80,176},{96,192},{112,... | collective-permute-start | bytes 294920 | tf_op jit(solution)/shard_map/ppermute | solution.py:27
  472.1 5.2 collective-permute-start.26
  477.3 5.1 collective-permute-start.27
  482.4 8.0 %collective-permute-start.28 = (f32[3,64,128]{2,1,0:T(8,128)S(1)}, f32[3,64,128]{2,1,0:T(8,128)S(1)}, u32[]{:S(2)}, u32[]{:S(2)}) collective-permute-start(f32[3,64,128]{2,1,0:T(8,128)S(1)} %get-tuple-element.16), channel_id=1, source_target_pairs={{0,144},{16,160},{32,176},{48,192},{64,208},{80,224},{96,240},{112... | collective-permute-start | bytes 294920 | tf_op jit(solution)/shard_map/ppermute | solution.py:27
  490.4 8.4 %collective-permute-start.29 = (f32[3,64,128]{2,1,0:T(8,128)S(1)}, f32[3,64,128]{2,1,0:T(8,128)S(1)}, u32[]{:S(2)}, u32[]{:S(2)}) collective-permute-start(f32[3,64,128]{2,1,0:T(8,128)S(1)} %get-tuple-element.15), channel_id=1, source_target_pairs={{0,160},{16,176},{32,192},{48,208},{64,224},{80,240},{96,0},{112,1... | collective-permute-start | bytes 294920 | tf_op jit(solution)/shard_map/ppermute | solution.py:27
  500.9 6.5 collective-permute-done.26
  509.3 14.0 %collective-permute-done.27 = f32[3,64,128]{2,1,0:T(8,128)S(1)} collective-permute-done((f32[3,64,128]{2,1,0:T(8,128)S(1)}, f32[3,64,128]{2,1,0:T(8,128)S(1)}, u32[]{:S(2)}, u32[]{:S(2)}) %collective-permute-start.27) | collective-permute-done | bytes 98336 | tf_op jit(solution)/shard_map/ppermute | solution.py:27
  530.8 5.6 collective-permute-done.30
  536.3 7.0 %collective-permute-done.31 = f32[3,64,128]{2,1,0:T(8,128)S(1)} collective-permute-done((f32[3,64,128]{2,1,0:T(8,128)S(1)}, f32[3,64,128]{2,1,0:T(8,128)S(1)}, u32[]{:S(2)}, u32[]{:S(2)}) %collective-permute-start.31) | collective-permute-done | bytes 98336 | tf_op jit(solution)/shard_map/ppermute | solution.py:27
  544.7 8.5 %collective-permute-done.33 = f32[3,64,128]{2,1,0:T(8,128)S(1)} collective-permute-done((f32[3,64,128]{2,1,0:T(8,128)S(1)}, f32[3,64,128]{2,1,0:T(8,128)S(1)}, u32[]{:S(2)}, u32[]{:S(2)}) %collective-permute-start.33) | collective-permute-done | bytes 98336 | tf_op jit(solution)/shard_map/ppermute | solution.py:27
  555.9 26.4 %all_to_all.95 = f32[48,64,128]{2,1,0:T(8,128)S(1)} all-to-all(f32[48,64,128]{2,1,0:T(8,128)S(1)} %bitcast.255), channel_id=1, replica_groups=mesh['phys'=2,'gx'=16,'gy'=16] {'gy'}, dimensions={0} | all-to-all | bytes 3145728 | tf_op jit(solution)/shard_map/all_to_all | solution.py:131
  593.5 5.4 reshape.216
  598.9 24.9 %all_to_all.96 = f32[16,1,24576]{2,1,0:T(1,128)S(1)} all-to-all(f32[16,1,24576]{2,1,0:T(1,128)S(1)} %reshape.216), channel_id=1, replica_groups=mesh['phys'=2,'gx'=16,'gy'=16] {'gy'}, dimensions={0} | all-to-all | bytes 3145728 | tf_op jit(solution)/shard_map/all_to_all | solution.py:129
  623.8 4.3 reduce.1
  642.2 5.4 collective-permute-start.37
  651.3 6.5 collective-permute-done.38
  (150 shorter events, 116.7 us)
Async XLA Ops:
  0.0 19.1 %copy-start = (f32[1,4,64,128]{3,2,1,0:T(8,128)S(1)}, f32[1,4,64,128]{3,2,1,0:T(8,128)}, u32[]{:S(2)}) copy-start(f32[1,4,64,128]{3,2,1,0:T(8,128)} %param.2) | copy-start | bytes 393220
  0.8 5.5 collective-permute-start
  2.1 4.9 collective-permute-start.1
  8.0 8.6 %collective-permute-start.2 = (f32[4,66,1]{2,1,0:T(8,128)S(1)}, f32[4,66,1]{2,1,0:T(8,128)S(1)}, u32[]{:S(2)}, u32[]{:S(2)}) collective-permute-start(f32[4,66,1]{2,1,0:T(8,128)S(1)} %get-tuple-element.54), channel_id=1, source_target_pairs={{1,0},{2,1},{3,2},{4,3},{5,4},{6,5},{7,6},{8,7},{9,8},{10,9},{11,1... | collective-permute-start | bytes 3176 | tf_op jit(solution)/shard_map/ppermute | solution.py:40
  11.6 6.2 collective-permute-start.3
  25.3 85.4 %all-to-all-start = ((f32[48,64,128]{2,1,0:T(8,128)}), f32[48,64,128]{2,1,0:T(8,128)S(1)}, u32[]{:S(2)}, u32[]{:S(2)}) async-start(f32[48,64,128]{2,1,0:T(8,128)} %reshape.181), calls=%async_computation | async-start | bytes 3145728 | tf_op jit(solution)/shard_map/all_to_all | solution.py:121
  42.0 188.9 %copy-start.1 = (s32[1024]{0:T(1024)}, s32[1024]{0:T(1024)S(1)}, u32[]{:S(2)}) copy-start(s32[1024]{0:T(1024)S(1)} %pad_clamp_fusion) | copy-start | bytes 12292
  117.5 21.6 %collective-permute-start.4 = (f32[3,64,128]{2,1,0:T(8,128)S(1)}, f32[3,64,128]{2,1,0:T(8,128)S(1)}, u32[]{:S(2)}, u32[]{:S(2)}) collective-permute-start(f32[3,64,128]{2,1,0:T(8,128)S(1)} %get-tuple-element.43), channel_id=1, source_target_pairs={{0,16},{16,32},{32,48},{48,64},{64,80},{80,96},{96,112},{112,128},... | collective-permute-start | bytes 294920 | tf_op jit(solution)/shard_map/ppermute | solution.py:27
  120.4 27.1 %collective-permute-start.5 = (f32[3,64,128]{2,1,0:T(8,128)S(1)}, f32[3,64,128]{2,1,0:T(8,128)S(1)}, u32[]{:S(2)}, u32[]{:S(2)}) collective-permute-start(f32[3,64,128]{2,1,0:T(8,128)S(1)} %get-tuple-element.42), channel_id=1, source_target_pairs={{0,32},{16,48},{32,64},{48,80},{64,96},{80,112},{96,128},{112,144}... | collective-permute-start | bytes 294920 | tf_op jit(solution)/shard_map/ppermute | solution.py:27
  125.1 28.1 %collective-permute-start.6 = (f32[3,64,128]{2,1,0:T(8,128)S(1)}, f32[3,64,128]{2,1,0:T(8,128)S(1)}, u32[]{:S(2)}, u32[]{:S(2)}) collective-permute-start(f32[3,64,128]{2,1,0:T(8,128)S(1)} %get-tuple-element.41), channel_id=1, source_target_pairs={{0,48},{16,64},{32,80},{48,96},{64,112},{80,128},{96,144},{112,160... | collective-permute-start | bytes 294920 | tf_op jit(solution)/shard_map/ppermute | solution.py:27
  131.0 28.6 %collective-permute-start.7 = (f32[3,64,128]{2,1,0:T(8,128)S(1)}, f32[3,64,128]{2,1,0:T(8,128)S(1)}, u32[]{:S(2)}, u32[]{:S(2)}) collective-permute-start(f32[3,64,128]{2,1,0:T(8,128)S(1)} %get-tuple-element.40), channel_id=1, source_target_pairs={{0,64},{16,80},{32,96},{48,112},{64,128},{80,144},{96,160},{112,17... | collective-permute-start | bytes 294920 | tf_op jit(solution)/shard_map/ppermute | solution.py:27
  137.1 29.2 %collective-permute-start.8 = (f32[3,64,128]{2,1,0:T(8,128)S(1)}, f32[3,64,128]{2,1,0:T(8,128)S(1)}, u32[]{:S(2)}, u32[]{:S(2)}) collective-permute-start(f32[3,64,128]{2,1,0:T(8,128)S(1)} %get-tuple-element.39), channel_id=1, source_target_pairs={{0,80},{16,96},{32,112},{48,128},{64,144},{80,160},{96,176},{112,1... | collective-permute-start | bytes 294920 | tf_op jit(solution)/shard_map/ppermute | solution.py:27
  139.1 36.6 %collective-permute-start.9 = (f32[3,64,128]{2,1,0:T(8,128)S(1)}, f32[3,64,128]{2,1,0:T(8,128)S(1)}, u32[]{:S(2)}, u32[]{:S(2)}) collective-permute-start(f32[3,64,128]{2,1,0:T(8,128)S(1)} %get-tuple-element.38), channel_id=1, source_target_pairs={{0,96},{16,112},{32,128},{48,144},{64,160},{80,176},{96,192},{112,... | collective-permute-start | bytes 294920 | tf_op jit(solution)/shard_map/ppermute | solution.py:27
  147.6 31.0 %collective-permute-start.10 = (f32[3,64,128]{2,1,0:T(8,128)S(1)}, f32[3,64,128]{2,1,0:T(8,128)S(1)}, u32[]{:S(2)}, u32[]{:S(2)}) collective-permute-start(f32[3,64,128]{2,1,0:T(8,128)S(1)} %get-tuple-element.37), channel_id=1, source_target_pairs={{0,112},{16,128},{32,144},{48,160},{64,176},{80,192},{96,208},{112... | collective-permute-start | bytes 294920 | tf_op jit(solution)/shard_map/ppermute | solution.py:27
  153.1 37.6 %collective-permute-start.11 = (f32[3,64,128]{2,1,0:T(8,128)S(1)}, f32[3,64,128]{2,1,0:T(8,128)S(1)}, u32[]{:S(2)}, u32[]{:S(2)}) collective-permute-start(f32[3,64,128]{2,1,0:T(8,128)S(1)} %get-tuple-element.36), channel_id=1, source_target_pairs={{0,128},{16,144},{32,160},{48,176},{64,192},{80,208},{96,224},{112... | collective-permute-start | bytes 294920 | tf_op jit(solution)/shard_map/ppermute | solution.py:27
  159.6 36.3 %collective-permute-start.12 = (f32[3,64,128]{2,1,0:T(8,128)S(1)}, f32[3,64,128]{2,1,0:T(8,128)S(1)}, u32[]{:S(2)}, u32[]{:S(2)}) collective-permute-start(f32[3,64,128]{2,1,0:T(8,128)S(1)} %get-tuple-element.35), channel_id=1, source_target_pairs={{0,144},{16,160},{32,176},{48,192},{64,208},{80,224},{96,240},{112... | collective-permute-start | bytes 294920 | tf_op jit(solution)/shard_map/ppermute | solution.py:27
  166.3 33.8 %collective-permute-start.13 = (f32[3,64,128]{2,1,0:T(8,128)S(1)}, f32[3,64,128]{2,1,0:T(8,128)S(1)}, u32[]{:S(2)}, u32[]{:S(2)}) collective-permute-start(f32[3,64,128]{2,1,0:T(8,128)S(1)} %get-tuple-element.34), channel_id=1, source_target_pairs={{0,160},{16,176},{32,192},{48,208},{64,224},{80,240},{96,0},{112,1... | collective-permute-start | bytes 294920 | tf_op jit(solution)/shard_map/ppermute | solution.py:27
  175.7 34.2 %collective-permute-start.14 = (f32[3,64,128]{2,1,0:T(8,128)S(1)}, f32[3,64,128]{2,1,0:T(8,128)S(1)}, u32[]{:S(2)}, u32[]{:S(2)}) collective-permute-start(f32[3,64,128]{2,1,0:T(8,128)S(1)} %get-tuple-element.33), channel_id=1, source_target_pairs={{0,176},{16,192},{32,208},{48,224},{64,240},{80,0},{96,16},{112,32... | collective-permute-start | bytes 294920 | tf_op jit(solution)/shard_map/ppermute | solution.py:27
  178.5 40.5 %collective-permute-start.15 = (f32[3,64,128]{2,1,0:T(8,128)S(1)}, f32[3,64,128]{2,1,0:T(8,128)S(1)}, u32[]{:S(2)}, u32[]{:S(2)}) collective-permute-start(f32[3,64,128]{2,1,0:T(8,128)S(1)} %get-tuple-element.32), channel_id=1, source_target_pairs={{0,192},{16,208},{32,224},{48,240},{64,0},{80,16},{96,32},{112,48}... | collective-permute-start | bytes 294920 | tf_op jit(solution)/shard_map/ppermute | solution.py:27
  190.7 33.7 %collective-permute-start.16 = (f32[3,64,128]{2,1,0:T(8,128)S(1)}, f32[3,64,128]{2,1,0:T(8,128)S(1)}, u32[]{:S(2)}, u32[]{:S(2)}) collective-permute-start(f32[3,64,128]{2,1,0:T(8,128)S(1)} %get-tuple-element.31), channel_id=1, source_target_pairs={{0,208},{16,224},{32,240},{48,0},{64,16},{80,32},{96,48},{112,64},... | collective-permute-start | bytes 294920 | tf_op jit(solution)/shard_map/ppermute | solution.py:27
  195.9 32.7 %collective-permute-start.17 = (f32[3,64,128]{2,1,0:T(8,128)S(1)}, f32[3,64,128]{2,1,0:T(8,128)S(1)}, u32[]{:S(2)}, u32[]{:S(2)}) collective-permute-start(f32[3,64,128]{2,1,0:T(8,128)S(1)} %get-tuple-element.30), channel_id=1, source_target_pairs={{0,224},{16,240},{32,0},{48,16},{64,32},{80,48},{96,64},{112,80},{... | collective-permute-start | bytes 294920 | tf_op jit(solution)/shard_map/ppermute | solution.py:27
  200.1 30.8 %collective-permute-start.18 = (f32[3,64,128]{2,1,0:T(8,128)S(1)}, f32[3,64,128]{2,1,0:T(8,128)S(1)}, u32[]{:S(2)}, u32[]{:S(2)}) collective-permute-start(f32[3,64,128]{2,1,0:T(8,128)S(1)} %get-tuple-element.29), channel_id=1, source_target_pairs={{0,240},{16,0},{32,16},{48,32},{64,48},{80,64},{96,80},{112,96},{1... | collective-permute-start | bytes 294920 | tf_op jit(solution)/shard_map/ppermute | solution.py:27
  232.7 28.3 %all-to-all-start.1 = ((f32[48,64,128]{2,1,0:T(8,128)}), f32[48,64,128]{2,1,0:T(8,128)S(1)}, u32[]{:S(2)}, u32[]{:S(2)}) async-start(f32[48,64,128]{2,1,0:T(8,128)} %bitcast.50), calls=%async_computation.1 | async-start | bytes 3145728 | tf_op jit(solution)/shard_map/all_to_all | solution.py:131
  310.6 7.9 %copy-start.2 = (f32[2,6]{1,0:T(2,128)S(1)}, f32[2,6]{1,0:T(2,128)}, u32[]{:S(2)}) copy-start(f32[2,6]{1,0:T(2,128)} %param.3) | copy-start | bytes 148
  314.0 39.2 %collective-permute-start.19 = (f32[48,64,128]{2,1,0:T(8,128)S(1)}, f32[48,64,128]{2,1,0:T(8,128)S(1)}, u32[]{:S(2)}, u32[]{:S(2)}) collective-permute-start(f32[48,64,128]{2,1,0:T(8,128)S(1)} %bitcast.253), channel_id=1, source_target_pairs={{0,256},{256,0},{1,257},{257,1},{2,258},{258,2},{3,259},{259,3},{4... | collective-permute-start | bytes 4718600 | tf_op jit(solution)/shard_map/ppermute | solution.py:52
  440.3 24.1 %collective-permute-start.20 = (f32[3,64,128]{2,1,0:T(8,128)S(1)}, f32[3,64,128]{2,1,0:T(8,128)S(1)}, u32[]{:S(2)}, u32[]{:S(2)}) collective-permute-start(f32[3,64,128]{2,1,0:T(8,128)S(1)} %get-tuple-element.24), channel_id=1, source_target_pairs={{0,16},{16,32},{32,48},{48,64},{64,80},{80,96},{96,112},{112,128},... | collective-permute-start | bytes 294920 | tf_op jit(solution)/shard_map/ppermute | solution.py:27
  445.3 26.8 %collective-permute-start.21 = (f32[3,64,128]{2,1,0:T(8,128)S(1)}, f32[3,64,128]{2,1,0:T(8,128)S(1)}, u32[]{:S(2)}, u32[]{:S(2)}) collective-permute-start(f32[3,64,128]{2,1,0:T(8,128)S(1)} %get-tuple-element.23), channel_id=1, source_target_pairs={{0,32},{16,48},{32,64},{48,80},{64,96},{80,112},{96,128},{112,144}... | collective-permute-start | bytes 294920 | tf_op jit(solution)/shard_map/ppermute | solution.py:27
  450.2 27.1 %collective-permute-start.22 = (f32[3,64,128]{2,1,0:T(8,128)S(1)}, f32[3,64,128]{2,1,0:T(8,128)S(1)}, u32[]{:S(2)}, u32[]{:S(2)}) collective-permute-start(f32[3,64,128]{2,1,0:T(8,128)S(1)} %get-tuple-element.22), channel_id=1, source_target_pairs={{0,48},{16,64},{32,80},{48,96},{64,112},{80,128},{96,144},{112,160... | collective-permute-start | bytes 294920 | tf_op jit(solution)/shard_map/ppermute | solution.py:27
  455.5 26.9 %collective-permute-start.23 = (f32[3,64,128]{2,1,0:T(8,128)S(1)}, f32[3,64,128]{2,1,0:T(8,128)S(1)}, u32[]{:S(2)}, u32[]{:S(2)}) collective-permute-start(f32[3,64,128]{2,1,0:T(8,128)S(1)} %get-tuple-element.21), channel_id=1, source_target_pairs={{0,64},{16,80},{32,96},{48,112},{64,128},{80,144},{96,160},{112,17... | collective-permute-start | bytes 294920 | tf_op jit(solution)/shard_map/ppermute | solution.py:27
  460.0 30.5 %collective-permute-start.24 = (f32[3,64,128]{2,1,0:T(8,128)S(1)}, f32[3,64,128]{2,1,0:T(8,128)S(1)}, u32[]{:S(2)}, u32[]{:S(2)}) collective-permute-start(f32[3,64,128]{2,1,0:T(8,128)S(1)} %get-tuple-element.20), channel_id=1, source_target_pairs={{0,80},{16,96},{32,112},{48,128},{64,144},{80,160},{96,176},{112,1... | collective-permute-start | bytes 294920 | tf_op jit(solution)/shard_map/ppermute | solution.py:27
  464.4 34.6 %collective-permute-start.25 = (f32[3,64,128]{2,1,0:T(8,128)S(1)}, f32[3,64,128]{2,1,0:T(8,128)S(1)}, u32[]{:S(2)}, u32[]{:S(2)}) collective-permute-start(f32[3,64,128]{2,1,0:T(8,128)S(1)} %get-tuple-element.19), channel_id=1, source_target_pairs={{0,96},{16,112},{32,128},{48,144},{64,160},{80,176},{96,192},{112,... | collective-permute-start | bytes 294920 | tf_op jit(solution)/shard_map/ppermute | solution.py:27
  472.1 35.3 %collective-permute-start.26 = (f32[3,64,128]{2,1,0:T(8,128)S(1)}, f32[3,64,128]{2,1,0:T(8,128)S(1)}, u32[]{:S(2)}, u32[]{:S(2)}) collective-permute-start(f32[3,64,128]{2,1,0:T(8,128)S(1)} %get-tuple-element.18), channel_id=1, source_target_pairs={{0,112},{16,128},{32,144},{48,160},{64,176},{80,192},{96,208},{112... | collective-permute-start | bytes 294920 | tf_op jit(solution)/shard_map/ppermute | solution.py:27
  477.3 46.0 %collective-permute-start.27 = (f32[3,64,128]{2,1,0:T(8,128)S(1)}, f32[3,64,128]{2,1,0:T(8,128)S(1)}, u32[]{:S(2)}, u32[]{:S(2)}) collective-permute-start(f32[3,64,128]{2,1,0:T(8,128)S(1)} %get-tuple-element.17), channel_id=1, source_target_pairs={{0,128},{16,144},{32,160},{48,176},{64,192},{80,208},{96,224},{112... | collective-permute-start | bytes 294920 | tf_op jit(solution)/shard_map/ppermute | solution.py:27
  482.4 42.8 %collective-permute-start.28 = (f32[3,64,128]{2,1,0:T(8,128)S(1)}, f32[3,64,128]{2,1,0:T(8,128)S(1)}, u32[]{:S(2)}, u32[]{:S(2)}) collective-permute-start(f32[3,64,128]{2,1,0:T(8,128)S(1)} %get-tuple-element.16), channel_id=1, source_target_pairs={{0,144},{16,160},{32,176},{48,192},{64,208},{80,224},{96,240},{112... | collective-permute-start | bytes 294920 | tf_op jit(solution)/shard_map/ppermute | solution.py:27
  490.4 36.7 %collective-permute-start.29 = (f32[3,64,128]{2,1,0:T(8,128)S(1)}, f32[3,64,128]{2,1,0:T(8,128)S(1)}, u32[]{:S(2)}, u32[]{:S(2)}) collective-permute-start(f32[3,64,128]{2,1,0:T(8,128)S(1)} %get-tuple-element.15), channel_id=1, source_target_pairs={{0,160},{16,176},{32,192},{48,208},{64,224},{80,240},{96,0},{112,1... | collective-permute-start | bytes 294920 | tf_op jit(solution)/shard_map/ppermute | solution.py:27
  498.9 37.4 %collective-permute-start.30 = (f32[3,64,128]{2,1,0:T(8,128)S(1)}, f32[3,64,128]{2,1,0:T(8,128)S(1)}, u32[]{:S(2)}, u32[]{:S(2)}) collective-permute-start(f32[3,64,128]{2,1,0:T(8,128)S(1)} %get-tuple-element.14), channel_id=1, source_target_pairs={{0,176},{16,192},{32,208},{48,224},{64,240},{80,0},{96,16},{112,32... | collective-permute-start | bytes 294920 | tf_op jit(solution)/shard_map/ppermute | solution.py:27
  507.4 36.0 %collective-permute-start.31 = (f32[3,64,128]{2,1,0:T(8,128)S(1)}, f32[3,64,128]{2,1,0:T(8,128)S(1)}, u32[]{:S(2)}, u32[]{:S(2)}) collective-permute-start(f32[3,64,128]{2,1,0:T(8,128)S(1)} %get-tuple-element.13), channel_id=1, source_target_pairs={{0,192},{16,208},{32,224},{48,240},{64,0},{80,16},{96,32},{112,48}... | collective-permute-start | bytes 294920 | tf_op jit(solution)/shard_map/ppermute | solution.py:27
  523.3 21.4 %collective-permute-start.32 = (f32[3,64,128]{2,1,0:T(8,128)S(1)}, f32[3,64,128]{2,1,0:T(8,128)S(1)}, u32[]{:S(2)}, u32[]{:S(2)}) collective-permute-start(f32[3,64,128]{2,1,0:T(8,128)S(1)} %get-tuple-element.12), channel_id=1, source_target_pairs={{0,208},{16,224},{32,240},{48,0},{64,16},{80,32},{96,48},{112,64},... | collective-permute-start | bytes 294920 | tf_op jit(solution)/shard_map/ppermute | solution.py:27
  525.2 28.0 %collective-permute-start.33 = (f32[3,64,128]{2,1,0:T(8,128)S(1)}, f32[3,64,128]{2,1,0:T(8,128)S(1)}, u32[]{:S(2)}, u32[]{:S(2)}) collective-permute-start(f32[3,64,128]{2,1,0:T(8,128)S(1)} %get-tuple-element.11), channel_id=1, source_target_pairs={{0,224},{16,240},{32,0},{48,16},{64,32},{80,48},{96,64},{112,80},{... | collective-permute-start | bytes 294920 | tf_op jit(solution)/shard_map/ppermute | solution.py:27
  527.2 27.9 %collective-permute-start.34 = (f32[3,64,128]{2,1,0:T(8,128)S(1)}, f32[3,64,128]{2,1,0:T(8,128)S(1)}, u32[]{:S(2)}, u32[]{:S(2)}) collective-permute-start(f32[3,64,128]{2,1,0:T(8,128)S(1)} %get-tuple-element.10), channel_id=1, source_target_pairs={{0,240},{16,0},{32,16},{48,32},{64,48},{80,64},{96,80},{112,96},{1... | collective-permute-start | bytes 294920 | tf_op jit(solution)/shard_map/ppermute | solution.py:27
  635.4 3.5 collective-permute-start.35
  637.7 4.4 collective-permute-start.36
  642.2 9.1 %collective-permute-start.37 = (f32[2,4,66,1]{3,2,1,0:T(8,128)S(1)}, f32[2,4,66,1]{3,2,1,0:T(8,128)S(1)}, u32[]{:S(2)}, u32[]{:S(2)}) collective-permute-start(f32[2,4,66,1]{3,2,1,0:T(8,128)S(1)} %get-tuple-element.46), channel_id=1, source_target_pairs={{0,1},{1,2},{2,3},{3,4},{4,5},{5,6},{6,7},{7,8},{8,9},{9,10},{10,1... | collective-permute-start | bytes 6344 | tf_op jit(solution)/shard_map/ppermute | solution.py:39
  647.6 10.2 %collective-permute-start.38 = (f32[2,4,66,1]{3,2,1,0:T(8,128)S(1)}, f32[2,4,66,1]{3,2,1,0:T(8,128)S(1)}, u32[]{:S(2)}, u32[]{:S(2)}) collective-permute-start(f32[2,4,66,1]{3,2,1,0:T(8,128)S(1)} %get-tuple-element.47), channel_id=1, source_target_pairs={{1,0},{2,1},{3,2},{4,3},{5,4},{6,5},{7,6},{8,7},{9,8},{10,9},{11,1... | collective-permute-start | bytes 6344 | tf_op jit(solution)/shard_map/ppermute | solution.py:40
